TPU v7x, 256 devices: a whole 4x4x8 slice. The times are simulated.
256 devices in a mesh: ctx: 16 (over y_hi, x, core), exp: 8 (over z), dp: 2 (over y_lo).
Axes of the slice: x: 4, y: 4 (y_hi: 2, y_lo: 2; y = y_hi * 2 + y_lo), z: 8, core: 2. Of those that a mesh axis runs over, the one named last changes fastest.
Arguments:
- tokens: bfloat16 [2, 2048, 4096], P('dp', 'ctx'), may hold values from -6 to 6
- norm_in: bfloat16 [4096], replicated, may hold values from 0.099609375 to 1.8984375
- w_qkv: bfloat16 [4096, 8, 6, 128], P('dp', 'exp')
- w_out: bfloat16 [8, 4, 128, 4096], P('exp', None, None, 'dp'), may hold values from -0.375 to 0.375
- norm_mid: bfloat16 [4096], replicated, may hold values from 0.099609375 to 1.8984375
- w_router: bfloat16 [4096, 8], replicated, may hold values from -0.09375 to 0.09375
- w_gate_up: bfloat16 [8, 4096, 2, 8192], P('exp', 'dp', None, 'ctx'), may hold values from -0.09375 to 0.09375
- w_down: bfloat16 [8, 8192, 4096], P('exp', 'ctx', 'dp'), may hold values from -0.0625 to 0.0625
- expert_ids: int32 [2, 2048, 2], P('dp', ('ctx', 'exp')), may hold values from 0 to 7, as said below
- slot_index: int32 [2, 2048, 2], P('dp', ('ctx', 'exp')), may hold values from 0 to 5, as said below
Outputs:
- layer_out: bfloat16 [2, 2048, 4096], P('dp', ('ctx', 'exp'))
Inputs may be any that keep to these rules, and one draw needn't show every extreme that they name: `expert_ids`: each token names two different experts; in every aligned block of 16 tokens (the tokens of one device) the numbers of choices of the experts are, in some order, 6, 5, 4, 4, 4, 3, 3 and 3, so that no expert is named more than 6 times and one exactly 6 times. `slot_index`: a choice's slot is the number of earlier choices of the same expert in its block of 16 tokens, a token's first choice counting before its second.
All inputs are finite; a program needn't handle non-finite values.
Results may differ from a plain program's by a relative error of at most 0.022.
The roundings to bfloat16 on the way count: a program that leaves them out, or rounds other values in their place, can miss the bound.
Values may be sent and summed in bfloat16 or wider, within the bound.
No kernel may reach another device: no remote copies, remote signals or barrier semaphores. Data moves between devices by JAX's collectives and lax.ppermute only.
A program may use at most 128 MiB of HBM per device.

v0:
```python
import math
import jax
import jax.numpy as jnp
from jax import lax
from jax.sharding import PartitionSpec as P

EPSILON = 1e-05
ROPE_BASE = 1000000.0


def rms_norm(values, gain):
    wide = values.astype(jnp.float32)
    square_mean = jnp.mean(wide * wide, axis=-1, keepdims=True)
    return (wide * lax.rsqrt(square_mean + EPSILON) * gain.astype(jnp.float32)).astype(jnp.bfloat16)


def rope_angles(positions, head_dim):
    half_dim = head_dim // 2
    freqs = jnp.exp(
        jnp.arange(half_dim, dtype=jnp.float32) * (-2.0 * math.log(ROPE_BASE) / head_dim)
    )
    return positions[:, None] * freqs[None, :]


def rotate(tensor, angles):
    half_dim = tensor.shape[-1] // 2
    first_half = tensor[..., :half_dim]
    second_half = tensor[..., half_dim:]
    cosine = jnp.cos(angles)
    sine = jnp.sin(angles)
    return jnp.concatenate(
        [first_half * cosine - second_half * sine, second_half * cosine + first_half * sine],
        axis=-1,
    )


def on_device(
    tokens, norm_in, w_qkv, w_out, norm_mid, w_router, w_gate_up, w_down, expert_ids, slot_index
):
    tok_rows = tokens.shape[1]
    head_dim = w_qkv.shape[3]
    kv_local = w_qkv.shape[1]
    group_size = w_qkv.shape[2] - 2
    width = tokens.shape[2]
    normed = rms_norm(tokens, norm_in)
    qkv_full, out_full, gate_up_all, down_all = (
        lax.all_gather(w_qkv, "dp", axis=0, tiled=True),
        lax.all_gather(w_out, "dp", axis=3, tiled=True),
        lax.all_gather(w_gate_up, "dp", axis=1, tiled=True),
        lax.all_gather(w_down, "dp", axis=2, tiled=True),
    )
    projected = jnp.dot(normed[0], qkv_full.reshape(width, -1), preferred_element_type=jnp.float32)[
        None
    ]
    projected = projected.reshape(1, tok_rows, kv_local, group_size + 2, head_dim)
    query_idx = lax.axis_index("ctx") * tok_rows + jnp.arange(tok_rows, dtype=jnp.int32)
    angles = rope_angles(query_idx.astype(jnp.float32), head_dim)
    queries = rotate(projected[:, :, :, :group_size, :], angles[None, :, None, None, :]).astype(
        jnp.bfloat16
    )
    keys_rot = rotate(projected[:, :, :, group_size, :], angles[None, :, None, :]).astype(
        jnp.bfloat16
    )
    values = projected[:, :, :, group_size + 1, :].astype(jnp.bfloat16)
    scale = 1.0 / math.sqrt(head_dim)
    last_query = lax.axis_index("ctx") * tok_rows + tok_rows - 1
    peak_init = jnp.full((1, kv_local, group_size, tok_rows), -1e30, jnp.float32)
    total_init = jnp.zeros((1, kv_local, group_size, tok_rows), jnp.float32)
    accum_init = jnp.zeros((1, kv_local, group_size, tok_rows, head_dim), jnp.float32)
    key_piece = lax.all_gather(keys_rot, "ctx", axis=1, tiled=True)
    value_piece = lax.all_gather(values, "ctx", axis=1, tiled=True)
    count = key_piece.shape[1]

    def compute(state):
        peak, totals, accum = state
        score_matrix = (
            jnp.einsum("bqkgd,bskd->bkgqs", queries, key_piece, preferred_element_type=jnp.float32)
            * scale
        )
        key_idx = jnp.arange(count, dtype=jnp.int32)
        causal = key_idx[None, :] <= query_idx[:, None]
        score_matrix = jnp.where(causal, score_matrix, -1e30)
        new_peak = jnp.maximum(peak, jnp.max(score_matrix, axis=-1))
        probs = jnp.where(causal, jnp.exp(score_matrix - new_peak[..., None]), 0.0)
        totals = jnp.sum(probs, axis=-1)
        update = jnp.einsum(
            "bkgqs,bskd->bkgqd",
            probs.astype(jnp.bfloat16),
            value_piece,
            preferred_element_type=jnp.float32,
        )
        accum = update
        return (new_peak, totals, accum)

    peak, totals, accum = lax.cond(
        jnp.int32(0) <= last_query,
        compute,
        lambda state: state,
        (peak_init, total_init, accum_init),
    )
    attended = jnp.transpose(accum / totals[..., None], (0, 3, 1, 2, 4)).astype(jnp.bfloat16)
    attended = attended.reshape(1, tok_rows, kv_local * group_size * head_dim)
    partial_sum = jnp.dot(
        attended[0], out_full.reshape(-1, width), preferred_element_type=jnp.float32
    )[None]
    head_total = lax.psum_scatter(
        partial_sum.astype(jnp.bfloat16), "exp", scatter_dimension=1, tiled=True
    ).astype(jnp.float32)
    rows = head_total.shape[1]
    own_tokens = lax.dynamic_slice_in_dim(tokens, lax.axis_index("exp") * rows, rows, 1)
    mixed = (own_tokens[0].astype(jnp.float32) + head_total[0]).astype(jnp.bfloat16)
    normed_mid = rms_norm(mixed, norm_mid)
    expert_count = w_router.shape[1]
    logits = jnp.dot(normed_mid, w_router, preferred_element_type=jnp.float32)
    choice_ids = expert_ids[0]
    picks = choice_ids[:, :, None] == jnp.arange(expert_count, dtype=jnp.int32)[None, None, :]
    chosen = jnp.sum(jnp.where(picks, logits[:, None, :], 0.0), axis=-1)
    gate_first = 1.0 / (1.0 + jnp.exp(chosen[:, 1] - chosen[:, 0]))
    gate_second = 1.0 - gate_first
    capacity = 6 * (rows // 16)
    exp_count = lax.axis_size("exp")
    exp_local = gate_up_all.shape[0]
    flat_index = choice_ids * capacity + slot_index[0]
    slot_cols = jnp.arange(expert_count * capacity, dtype=jnp.int32)
    placer = jnp.logical_or(
        slot_cols[:, None] == flat_index[None, :, 0], slot_cols[:, None] == flat_index[None, :, 1]
    ).astype(jnp.bfloat16)
    buffer_rows = jnp.dot(placer, normed_mid, preferred_element_type=jnp.float32).astype(
        jnp.bfloat16
    )
    buffer_rows = buffer_rows.reshape(exp_count, exp_local, capacity, width)
    received = lax.all_to_all(buffer_rows, "exp", split_axis=0, concat_axis=0, tiled=True)
    gathered_rows = lax.all_gather(received[None], "ctx", axis=0, tiled=True)
    gate_up_vals = jnp.einsum(
        "cnlrd,ldjf->cnlrjf", gathered_rows, gate_up_all, preferred_element_type=jnp.float32
    )
    hidden = (jax.nn.silu(gate_up_vals[..., 0, :]) * gate_up_vals[..., 1, :]).astype(jnp.bfloat16)
    summed_result = lax.psum_scatter(
        jnp.einsum("cnlrf,lfd->cnlrd", hidden, down_all, preferred_element_type=jnp.float32).astype(
            jnp.bfloat16
        ),
        "ctx",
        scatter_dimension=0,
        tiled=True,
    ).astype(jnp.float32)
    expert_out = summed_result[0].astype(jnp.bfloat16)
    returned = lax.all_to_all(expert_out, "exp", split_axis=0, concat_axis=0, tiled=True)
    returned = returned.reshape(expert_count * capacity, width)
    combiner = gate_first[:, None] * (flat_index[:, 0:1] == slot_cols[None, :]).astype(
        jnp.float32
    ) + gate_second[:, None] * (flat_index[:, 1:2] == slot_cols[None, :]).astype(jnp.float32)
    moe_total = jnp.dot(combiner, returned.astype(jnp.float32), precision=lax.Precision.HIGHEST)
    return (mixed.astype(jnp.float32) + moe_total).astype(jnp.bfloat16)[None]


def solution(mesh):
    placed = (
        P("dp", "ctx", None),
        P(),
        P("dp", "exp", None, None),
        P("exp", None, None, "dp"),
        P(),
        P(),
        P("exp", "dp", None, "ctx"),
        P("exp", "ctx", "dp"),
        P("dp", ("ctx", "exp"), None),
        P("dp", ("ctx", "exp"), None),
    )
    return jax.shard_map(
        on_device,
        mesh=mesh,
        in_specs=placed,
        out_specs=P("dp", ("ctx", "exp"), None),
        check_vma=False,
    )
```

profile of v0, /device:TPU:2, one launch (start us, length us, event | category | flops | bytes accessed | tf_op | source)
XLA Modules:
  0.0 595.8 jit_solution(7468417833645752006)
XLA Ops:
  6.5 4.8 copy.44
  13.1 86.9 %all-gather.8.cloned.1.call-done = bf16[4096,1,6,128]{0,3,2,1:T(8,128)(2,1)} async-done(((bf16[2048,1,6,128]{0,3,2,1:T(8,128)(2,1)}), bf16[4096,1,6,128]{0,3,2,1:T(8,128)(2,1)}) %all-gather.8.cloned.1.call-update) | async-done | bytes 6291472 | tf_op jit(solution)/shard_map/all_gather | solution.py:47
  99.9 4.6 fusion.36
  104.9 21.1 %all_gather.22 = bf16[1,2048,1,128]{1,3,2,0:T(8,128)(2,1)S(1)} all-gather(bf16[1,128,1,128]{1,3,2,0:T(8,128)(2,1)S(1)} %pad_maximum_fusion.1), channel_id=1, replica_groups=mesh['ctx'=16,'exp'=8,'dp'=2] {'ctx'}, dimensions={1}, use_global_device_ids=true | all-gather | bytes 557056 | tf_op jit(solution)/shard_map/all_gather | solution.py:70
  126.0 25.5 %all-gather = bf16[1,2048,1,1,128]{1,4,3,2,0:T(8,128)(2,1)S(1)} all-gather(bf16[1,128,1,1,128]{1,4,3,2,0:T(8,128)(2,1)S(1)} %slice.86), channel_id=2, replica_groups=mesh['ctx'=16,'exp'=8,'dp'=2] {'ctx'}, dimensions={1}, use_global_device_ids=true | all-gather | bytes 557056 | tf_op jit(solution)/shard_map/all_gather | solution.py:71
  151.4 3.1 conditional.1
  152.4 1.1 fusion.7
  153.5 1.0 fusion.2
  154.5 10.0 %all-gather.10.cloned.1.call-done = bf16[1,4,128,4096]{3,2,1,0:T(8,128)(2,1)} async-done(((bf16[1,4,128,2048]{3,2,1,0:T(8,128)(2,1)}), bf16[1,4,128,4096]{3,2,1,0:T(8,128)(2,1)}) %all-gather.10.cloned.1.call-update) | async-done | bytes 4194320 | tf_op jit(solution)/shard_map/all_gather | solution.py:48
  164.6 3.9 fusion.23
  168.6 4.9 copy.51
  174.2 36.3 %reduce-scatter.3.cloned.1.call-done = bf16[1,16,4096]{2,1,0:T(8,128)(2,1)} async-done(((bf16[1,128,4096]{2,1,0:T(8,128)(2,1)}), bf16[1,16,4096]{2,1,0:T(8,128)(2,1)}) %reduce-scatter.3.cloned.1.call-update) | async-done | bytes 131088 | tf_op jit(solution)/shard_map/reduce_scatter | solution.py:106
  210.5 1.1 fusion.45
  212.0 17.6 %all_to_all.10 = bf16[8,1,6,4096]{3,2,1,0:T(8,128)(2,1)S(1)} all-to-all(bf16[8,1,6,4096]{3,2,1,0:T(8,128)(2,1)S(1)} %bitcast.132), channel_id=1, replica_groups=mesh['ctx'=16,'exp'=8,'dp'=2] {'exp'}, dimensions={0} | all-to-all | bytes 786432 | tf_op jit(solution)/shard_map/all_to_all | solution.py:132
  231.4 88.6 %all-gather.12.cloned.1.call-done = bf16[1,4096,2,512]{3,1,2,0:T(8,128)(2,1)} async-done(((bf16[1,2048,2,512]{3,1,2,0:T(8,128)(2,1)}), bf16[1,4096,2,512]{3,1,2,0:T(8,128)(2,1)}) %all-gather.12.cloned.1.call-update) | async-done | bytes 8388624 | tf_op jit(solution)/shard_map/all_gather | solution.py:49
  320.0 72.3 %all-gather.16.cloned.1.call-done = bf16[128,1,6,4096]{3,0,2,1:T(8,128)(2,1)} async-done(((bf16[8,1,6,4096]{3,0,2,1:T(8,128)(2,1)}), bf16[128,1,6,4096]{3,0,2,1:T(8,128)(2,1)}) %all-gather.16.cloned.1.call-update) | async-done | bytes 6291472 | tf_op jit(solution)/shard_map/all_gather | solution.py:133
  392.3 12.1 %fusion.30 = f32[16,8,1,6,2,512]{5,1,4,3,0,2:T(8,128)} fusion(bf16[1,4096,2,512]{3,1,2,0:T(8,128)(2,1)} %all-gather.12.cloned.1.call-done, bf16[128,1,6,4096]{3,0,2,1:T(8,128)(2,1)} %all-gather.16.cloned.1.call-done), kind=kOutput, calls=%fused_computation.38 | convolution fusion | flops 6442450944 | bytes 17825792 | tf_op jit(solution)/shard_map/cnlrd,ldjf->cnlrjf/dot_general | solution.py:134
  404.4 50.6 %all-gather.14.cloned.1.call-done = bf16[1,512,4096]{2,1,0:T(8,128)(2,1)} async-done(((bf16[1,512,2048]{2,1,0:T(8,128)(2,1)}), bf16[1,512,4096]{2,1,0:T(8,128)(2,1)}) %all-gather.14.cloned.1.call-update) | async-done | bytes 4194320 | tf_op jit(solution)/shard_map/all_gather | solution.py:50
  455.0 9.2 %fusion.22 = bf16[16,8,1,6,4096]{4,1,3,0,2:T(8,128)(2,1)} fusion(bf16[1,512,4096]{2,1,0:T(8,128)(2,1)} %all-gather.14.cloned.1.call-done, f32[16,8,1,6,2,512]{5,1,4,3,0,2:T(8,128)} %fusion.30), kind=kOutput, calls=%fused_computation.25 | convolution fusion | flops 3226730496 | bytes 13631488 | tf_op jit(solution)/shard_map/cnlrf,lfd->cnlrd/dot_general | solution.py:139
  464.3 98.2 %reduce-scatter.5.cloned.1.call-done = bf16[1,8,1,6,4096]{4,1,3,0,2:T(8,128)(2,1)} async-done(((bf16[16,8,1,6,4096]{4,1,3,0,2:T(8,128)(2,1)}), bf16[1,8,1,6,4096]{4,1,3,0,2:T(8,128)(2,1)}) %reduce-scatter.5.cloned.1.call-update) | async-done | bytes 393232 | tf_op jit(solution)/shard_map/reduce_scatter | solution.py:138
  562.5 2.0 copy.53
  564.5 7.0 %all-to-all-start.1 = ((bf16[8,1,6,4096]{3,2,1,0:T(8,128)(2,1)}), bf16[8,1,6,4096]{3,2,1,0:T(8,128)(2,1)S(1)}, u32[]{:S(2)}, u32[]{:S(2)}) async-start(bf16[8,1,6,4096]{3,2,1,0:T(8,128)(2,1)} %copy.53), calls=%async_computation.3 | async-start | bytes 1048576 | tf_op jit(solution)/shard_map/all_to_all | solution.py:147
  571.8 16.1 %all-to-all-done.1 = bf16[8,1,6,4096]{3,2,1,0:T(8,128)(2,1)S(1)} async-done(((bf16[8,1,6,4096]{3,2,1,0:T(8,128)(2,1)}), bf16[8,1,6,4096]{3,2,1,0:T(8,128)(2,1)S(1)}, u32[]{:S(2)}, u32[]{:S(2)}) %all-to-all-start.1) | async-done | bytes 393248 | tf_op jit(solution)/shard_map/all_to_all | solution.py:147
  588.0 1.0 fusion.25
  (55 shorter events, 6.4 us)
Async XLA Ops:
  6.5 565.0 %copy-start = (bf16[4096,8]{0,1:T(8,128)(2,1)S(1)}, bf16[4096,8]{0,1:T(8,128)(2,1)}, u32[]{:S(2)}) copy-start(bf16[4096,8]{0,1:T(8,128)(2,1)} %param.17) | copy-start | bytes 196612
  6.5 93.4 %all-gather.8.cloned.1.call-start = ((), (), s32[]{:S(2)}) async-start(), calls=%async_computation.4 | async-start | bytes 9437184 | tf_op jit(solution)/shard_map/all_gather | solution.py:47
  11.3 0.8 copy-start.2
  11.3 1.2 copy-start.1
  11.3 153.2 %all-gather.10.cloned.1.call-start = ((), (), s32[]{:S(2)}) async-start(), calls=%async_computation.5 | async-start | bytes 6291456 | tf_op jit(solution)/shard_map/all_gather | solution.py:48
  12.1 198.4 %reduce-scatter.3.cloned.1.call-start = ((), (), s32[]{:S(2)}) async-start(), calls=%async_computation.6 | async-start | bytes 1179648 | tf_op jit(solution)/shard_map/reduce_scatter | solution.py:106
  168.5 151.5 %all-gather.12.cloned.1.call-start = ((), (), s32[]{:S(2)}) async-start(), calls=%async_computation.7 | async-start | bytes 12582912 | tf_op jit(solution)/shard_map/all_gather | solution.py:49
  173.5 0.7 copy-start.3
  173.5 0.7 copy-start.4
  173.5 0.7 copy-start.5
  173.5 218.9 %all-gather.16.cloned.1.call-start = ((), (), s32[]{:S(2)}) async-start(), calls=%async_computation.10 | async-start | bytes 6684672 | tf_op jit(solution)/shard_map/all_gather | solution.py:133
  230.6 224.4 %all-gather.14.cloned.1.call-start = ((), (), s32[]{:S(2)}) async-start(), calls=%async_computation.8 | async-start | bytes 6291456 | tf_op jit(solution)/shard_map/all_gather | solution.py:50
  231.2 331.3 %reduce-scatter.5.cloned.1.call-start = ((), (), s32[]{:S(2)}) async-start(), calls=%async_computation.9 | async-start | bytes 6684672 | tf_op jit(solution)/shard_map/reduce_scatter | solution.py:138
  564.5 23.4 %all-to-all-start.1 = ((bf16[8,1,6,4096]{3,2,1,0:T(8,128)(2,1)}), bf16[8,1,6,4096]{3,2,1,0:T(8,128)(2,1)S(1)}, u32[]{:S(2)}, u32[]{:S(2)}) async-start(bf16[8,1,6,4096]{3,2,1,0:T(8,128)(2,1)} %copy.53), calls=%async_computation.3 | async-start | bytes 1048576 | tf_op jit(solution)/shard_map/all_to_all | solution.py:147
Sparse Core Ops, SparseCore 0:
  11.5 88.4 all-gather.7
  101.7 62.8 all-gather.9
  168.6 41.8 reduce-scatter.2
  212.2 107.8 all-gather.11
  322.7 69.6 all-gather.15
  394.0 60.9 all-gather.13
  464.4 98.0 reduce-scatter.4
where the time goes:
time: 596 us
  waiting for transfers between devices  460 us (77%)
  blocking collectives  64.1 us (11%)
  matrix products  33.3 us (6%)
  local copies, waits for them, and re-layouts  14 us (2%)
  between operations  13.7 us (2%)
  starting transfers between devices  7.44 us (1%)
    reduce_scatter x1, waiting for transfers between devices, on_device(): lax.psum_scatter(jnp.einsum('cnlrf,lfd->cnlrd', hidden, down_all, preferr...  98.2 us
    all_gather x1, waiting for transfers between devices, on_device(): lax.all_gather(w_gate_up, 'dp', axis=1, tiled=True)  88.6 us
    all_gather x1, waiting for transfers between devices, on_device(): lax.all_gather(w_qkv, 'dp', axis=0, tiled=True)  86.9 us
    all_gather x1, waiting for transfers between devices, on_device(): gathered_rows = lax.all_gather(received[None], 'ctx', axis=0, tiled=True)  72.3 us
    all_gather x1, waiting for transfers between devices, on_device(): lax.all_gather(w_down, 'dp', axis=2, tiled=True)  50.6 us
    reduce_scatter x1, waiting for transfers between devices, on_device(): lax.psum_scatter(partial_sum.astype(jnp.bfloat16), 'exp', scatter_dimensi...  36.3 us
    all_gather x1, blocking collectives, on_device(): value_piece = lax.all_gather(values, 'ctx', axis=1, tiled=True)  25.5 us
    all_gather x1, blocking collectives, on_device(): key_piece = lax.all_gather(keys_rot, 'ctx', axis=1, tiled=True)  21.1 us
  transfers between devices with their start and end apart: 8, of which 8 were waited for; matrix products, arithmetic and copies ran while one was open for 5% of the time, Pallas kernels for 0%

commit v1 on v0

--- a/solution.py
+++ b/solution.py
@@ -67,8 +67,11 @@
     peak_init = jnp.full((1, kv_local, group_size, tok_rows), -1e30, jnp.float32)
     total_init = jnp.zeros((1, kv_local, group_size, tok_rows), jnp.float32)
     accum_init = jnp.zeros((1, kv_local, group_size, tok_rows, head_dim), jnp.float32)
-    key_piece = lax.all_gather(keys_rot, "ctx", axis=1, tiled=True)
-    value_piece = lax.all_gather(values, "ctx", axis=1, tiled=True)
+    key_piece, value_piece = jnp.split(
+        lax.all_gather(jnp.concatenate([keys_rot, values], axis=0), "ctx", axis=1, tiled=True),
+        [keys_rot.shape[0]],
+        axis=0,
+    )
     count = key_piece.shape[1]
 
     def compute(state):

time: 596 us -> 650 us (1.091)
  waiting for transfers between devices: 460 us -> 558 us
  blocking collectives: 64.1 us -> 17.7 us
    all_gather x0 -> x1, waiting for transfers between devices: none -> 50.2 us  [on_device(): lax.all_gather(jnp.concatenate([keys_rot, values], axis=0), 'ctx', axis=1...]
    all_gather x1, waiting for transfers between devices: 10 us -> 58.1 us  [on_device(): lax.all_gather(w_out, 'dp', axis=3, tiled=True)]
    all_gather x2 -> x0, blocking collectives: 46.6 us -> none  [the longest x1 25.5 us: on_device(): value_piece = lax.all_gather(values, 'ctx', axis=1, tiled=True)]
  transfers between devices with their start and end apart: 8 -> 9, of which waited for: 8 -> 9; matrix products, arithmetic and copies ran while one was open for 5% -> 4% of each run, Pallas kernels for 0% -> 0%
where the time goes in v1:
time: 650 us; the launch traced here: 649 us
  waiting for transfers between devices  558 us (86%)
  matrix products  33.3 us (5%)
  blocking collectives  17.7 us (3%)
  local copies, waits for them, and re-layouts  15.3 us (2%)
  between operations  13.7 us (2%)
  starting transfers between devices  7.48 us (1%)
    reduce_scatter x1, waiting for transfers between devices, on_device(): lax.psum_scatter(jnp.einsum('cnlrf,lfd->cnlrd', hidden, down_all, preferr...  98.2 us
    all_gather x1, waiting for transfers between devices, on_device(): lax.all_gather(w_gate_up, 'dp', axis=1, tiled=True)  88.3 us
    all_gather x1, waiting for transfers between devices, on_device(): lax.all_gather(w_qkv, 'dp', axis=0, tiled=True)  88.2 us
    all_gather x1, waiting for transfers between devices, on_device(): gathered_rows = lax.all_gather(received[None], 'ctx', axis=0, tiled=True)  72.3 us
    all_gather x1, waiting for transfers between devices, on_device(): lax.all_gather(w_out, 'dp', axis=3, tiled=True)  58.1 us
    all_gather x1, waiting for transfers between devices, on_device(): lax.all_gather(w_down, 'dp', axis=2, tiled=True)  50.7 us
    all_gather x1, waiting for transfers between devices, on_device(): lax.all_gather(jnp.concatenate([keys_rot, values], axis=0), 'ctx', axis=1...  50.2 us
    reduce_scatter x1, waiting for transfers between devices, on_device(): lax.psum_scatter(partial_sum.astype(jnp.bfloat16), 'exp', scatter_dimensi...  34.2 us
  transfers between devices with their start and end apart: 9, of which 9 were waited for; matrix products, arithmetic and copies ran while one was open for 4% of the time, Pallas kernels for 0%

profile of v1, /device:TPU:2, one launch (start us, length us, event | category | flops | bytes accessed | tf_op | source)
XLA Modules:
  0.0 649.0 jit_solution(14449052659741877538)
XLA Ops:
  6.5 4.9 copy.41
  11.9 88.2 %all-gather.8.cloned.1.call-done = bf16[4096,1,6,128]{0,3,2,1:T(8,128)(2,1)} async-done(((bf16[2048,1,6,128]{0,3,2,1:T(8,128)(2,1)}), bf16[4096,1,6,128]{0,3,2,1:T(8,128)(2,1)}) %all-gather.8.cloned.1.call-update) | async-done | bytes 6291472 | tf_op jit(solution)/shard_map/all_gather | solution.py:47
  100.0 4.6 fusion.34
  106.6 50.2 %all-gather.10.cloned.1.call-done = bf16[2,2048,1,128]{1,3,2,0:T(8,128)(2,1)} async-done(((bf16[2,128,1,128]{1,3,2,0:T(8,128)(2,1)}), bf16[2,2048,1,128]{1,3,2,0:T(8,128)(2,1)}) %all-gather.10.cloned.1.call-update) | async-done | bytes 1048592 | tf_op jit(solution)/shard_map/all_gather | solution.py:71
  156.9 4.6 conditional.1
  157.1 1.6 copy.42
  159.4 1.1 fusion.7
  160.5 1.0 fusion.2
  161.5 58.1 %all-gather.12.cloned.1.call-done = bf16[1,4,128,4096]{3,2,1,0:T(8,128)(2,1)} async-done(((bf16[1,4,128,2048]{3,2,1,0:T(8,128)(2,1)}), bf16[1,4,128,4096]{3,2,1,0:T(8,128)(2,1)}) %all-gather.12.cloned.1.call-update) | async-done | bytes 4194320 | tf_op jit(solution)/shard_map/all_gather | solution.py:48
  219.7 4.0 fusion.21
  223.8 4.9 copy.47
  229.4 34.2 %reduce-scatter.3.cloned.1.call-done = bf16[1,16,4096]{2,1,0:T(8,128)(2,1)} async-done(((bf16[1,128,4096]{2,1,0:T(8,128)(2,1)}), bf16[1,16,4096]{2,1,0:T(8,128)(2,1)}) %reduce-scatter.3.cloned.1.call-update) | async-done | bytes 131088 | tf_op jit(solution)/shard_map/reduce_scatter | solution.py:109
  263.6 1.1 fusion.43
  265.1 17.7 %all_to_all.10 = bf16[8,1,6,4096]{3,2,1,0:T(8,128)(2,1)S(1)} all-to-all(bf16[8,1,6,4096]{3,2,1,0:T(8,128)(2,1)S(1)} %bitcast.131), channel_id=1, replica_groups=mesh['ctx'=16,'exp'=8,'dp'=2] {'exp'}, dimensions={0} | all-to-all | bytes 786432 | tf_op jit(solution)/shard_map/all_to_all | solution.py:135
  284.7 88.3 %all-gather.14.cloned.1.call-done = bf16[1,4096,2,512]{3,1,2,0:T(8,128)(2,1)} async-done(((bf16[1,2048,2,512]{3,1,2,0:T(8,128)(2,1)}), bf16[1,4096,2,512]{3,1,2,0:T(8,128)(2,1)}) %all-gather.14.cloned.1.call-update) | async-done | bytes 8388624 | tf_op jit(solution)/shard_map/all_gather | solution.py:49
  373.1 72.3 %all-gather.18.cloned.1.call-done = bf16[128,1,6,4096]{3,0,2,1:T(8,128)(2,1)} async-done(((bf16[8,1,6,4096]{3,0,2,1:T(8,128)(2,1)}), bf16[128,1,6,4096]{3,0,2,1:T(8,128)(2,1)}) %all-gather.18.cloned.1.call-update) | async-done | bytes 6291472 | tf_op jit(solution)/shard_map/all_gather | solution.py:136
  445.4 12.1 %fusion.28 = f32[16,8,1,6,2,512]{5,1,4,3,0,2:T(8,128)} fusion(bf16[1,4096,2,512]{3,1,2,0:T(8,128)(2,1)} %all-gather.14.cloned.1.call-done, bf16[128,1,6,4096]{3,0,2,1:T(8,128)(2,1)} %all-gather.18.cloned.1.call-done), kind=kOutput, calls=%fused_computation.38 | convolution fusion | flops 6442450944 | bytes 17825792 | tf_op jit(solution)/shard_map/cnlrd,ldjf->cnlrjf/dot_general | solution.py:137
  457.5 50.7 %all-gather.16.cloned.1.call-done = bf16[1,512,4096]{2,1,0:T(8,128)(2,1)} async-done(((bf16[1,512,2048]{2,1,0:T(8,128)(2,1)}), bf16[1,512,4096]{2,1,0:T(8,128)(2,1)}) %all-gather.16.cloned.1.call-update) | async-done | bytes 4194320 | tf_op jit(solution)/shard_map/all_gather | solution.py:50
  508.2 9.2 %fusion.20 = bf16[16,8,1,6,4096]{4,1,3,0,2:T(8,128)(2,1)} fusion(bf16[1,512,4096]{2,1,0:T(8,128)(2,1)} %all-gather.16.cloned.1.call-done, f32[16,8,1,6,2,512]{5,1,4,3,0,2:T(8,128)} %fusion.28), kind=kOutput, calls=%fused_computation.25 | convolution fusion | flops 3226730496 | bytes 13631488 | tf_op jit(solution)/shard_map/cnlrf,lfd->cnlrd/dot_general | solution.py:142
  517.4 98.2 %reduce-scatter.5.cloned.1.call-done = bf16[1,8,1,6,4096]{4,1,3,0,2:T(8,128)(2,1)} async-done(((bf16[16,8,1,6,4096]{4,1,3,0,2:T(8,128)(2,1)}), bf16[1,8,1,6,4096]{4,1,3,0,2:T(8,128)(2,1)}) %reduce-scatter.5.cloned.1.call-update) | async-done | bytes 393232 | tf_op jit(solution)/shard_map/reduce_scatter | solution.py:141
  615.6 2.0 copy.49
  617.7 7.0 %all-to-all-start.1 = ((bf16[8,1,6,4096]{3,2,1,0:T(8,128)(2,1)}), bf16[8,1,6,4096]{3,2,1,0:T(8,128)(2,1)S(1)}, u32[]{:S(2)}, u32[]{:S(2)}) async-start(bf16[8,1,6,4096]{3,2,1,0:T(8,128)(2,1)} %copy.49), calls=%async_computation.3 | async-start | bytes 1048576 | tf_op jit(solution)/shard_map/all_to_all | solution.py:150
  624.9 16.1 %all-to-all-done.1 = bf16[8,1,6,4096]{3,2,1,0:T(8,128)(2,1)S(1)} async-done(((bf16[8,1,6,4096]{3,2,1,0:T(8,128)(2,1)}), bf16[8,1,6,4096]{3,2,1,0:T(8,128)(2,1)S(1)}, u32[]{:S(2)}, u32[]{:S(2)}) %all-to-all-start.1) | async-done | bytes 393248 | tf_op jit(solution)/shard_map/all_to_all | solution.py:150
  641.2 1.0 fusion.23
  (57 shorter events, 6.8 us)
Async XLA Ops:
  6.5 618.1 %copy-start = (bf16[4096,8]{0,1:T(8,128)(2,1)S(1)}, bf16[4096,8]{0,1:T(8,128)(2,1)}, u32[]{:S(2)}) copy-start(bf16[4096,8]{0,1:T(8,128)(2,1)} %param.17) | copy-start | bytes 196612
  6.5 5.0 copy-start.2
  6.5 5.0 copy-start.1
  6.5 93.5 %all-gather.8.cloned.1.call-start = ((), (), s32[]{:S(2)}) async-start(), calls=%async_computation.4 | async-start | bytes 9437184 | tf_op jit(solution)/shard_map/all_gather | solution.py:47
  11.4 145.4 %all-gather.10.cloned.1.call-start = ((), (), s32[]{:S(2)}) async-start(), calls=%async_computation.5 | async-start | bytes 1114112 | tf_op jit(solution)/shard_map/all_gather | solution.py:71
  105.6 114.1 %all-gather.12.cloned.1.call-start = ((), (), s32[]{:S(2)}) async-start(), calls=%async_computation.6 | async-start | bytes 6291456 | tf_op jit(solution)/shard_map/all_gather | solution.py:48
  106.3 157.2 %reduce-scatter.3.cloned.1.call-start = ((), (), s32[]{:S(2)}) async-start(), calls=%async_computation.7 | async-start | bytes 1179648 | tf_op jit(solution)/shard_map/reduce_scatter | solution.py:109
  223.7 149.3 %all-gather.14.cloned.1.call-start = ((), (), s32[]{:S(2)}) async-start(), calls=%async_computation.8 | async-start | bytes 12582912 | tf_op jit(solution)/shard_map/all_gather | solution.py:49
  228.7 0.7 copy-start.3
  228.7 0.7 copy-start.4
  228.7 0.7 copy-start.5
  228.7 216.7 %all-gather.18.cloned.1.call-start = ((), (), s32[]{:S(2)}) async-start(), calls=%async_computation.11 | async-start | bytes 6684672 | tf_op jit(solution)/shard_map/all_gather | solution.py:136
  283.8 224.4 %all-gather.16.cloned.1.call-start = ((), (), s32[]{:S(2)}) async-start(), calls=%async_computation.9 | async-start | bytes 6291456 | tf_op jit(solution)/shard_map/all_gather | solution.py:50
  284.5 331.1 %reduce-scatter.5.cloned.1.call-start = ((), (), s32[]{:S(2)}) async-start(), calls=%async_computation.10 | async-start | bytes 6684672 | tf_op jit(solution)/shard_map/reduce_scatter | solution.py:141
  617.7 23.4 %all-to-all-start.1 = ((bf16[8,1,6,4096]{3,2,1,0:T(8,128)(2,1)}), bf16[8,1,6,4096]{3,2,1,0:T(8,128)(2,1)S(1)}, u32[]{:S(2)}, u32[]{:S(2)}) async-start(bf16[8,1,6,4096]{3,2,1,0:T(8,128)(2,1)} %copy.49), calls=%async_computation.3 | async-start | bytes 1048576 | tf_op jit(solution)/shard_map/all_to_all | solution.py:150
Sparse Core Ops, SparseCore 0:
  11.6 88.4 all-gather.7
  105.7 51.1 all-gather.9
  158.7 60.9 all-gather.11
  223.8 39.6 reduce-scatter.2
  265.2 107.8 all-gather.13
  375.7 69.6 all-gather.17
  447.2 60.9 all-gather.15
  517.6 98.0 reduce-scatter.4
